TPU v7x, 512 devices: a whole 4x8x8 slice. The times are simulated.
512 devices in a mesh: amp: 8 (over y), int: 16 (over z, core), rep: 4 (over x).
Axes of the slice: x: 4, y: 8, z: 8, core: 2. Of those that a mesh axis runs over, the one named last changes fastest.
Arguments:
- amplitudes: bfloat16 [32, 1024, 4096], P('int', 'amp', 'rep'), may hold values from -6 to 6
- pp_blocks: bfloat16 [4, 128, 128, 128], P('rep', 'int'), may hold values from -0.5 to 0.5
- src_tiles: int32 [4, 128], P('rep', 'int'), may hold values from 0 to 7
- src_wins: int32 [4, 128], P('rep', 'int'), may hold values from 0 to 31
- dst_tiles: int32 [4, 128], P('rep', 'int'), may hold values from 0 to 31
- dst_wins: int32 [4, 128], P('rep', 'int'), may hold values from 0 to 1
- hh_integrals: bfloat16 [1024, 1024], replicated, may hold values from -0.1875 to 0.1875
- pair_gap: float32 [1024], P('amp'), may hold values from 0.5 to 2
- vir_energy: float32 [4096], P('rep'), may hold values from 0.5 to 2
- win_energy: float32 [32], P('int'), may hold values from 0.5 to 2
Outputs:
- amp_update: float32 [32, 1024, 4096], P('int', 'amp', 'rep')
Inputs may be any that keep to these rules, and one draw needn't show every extreme that they name: `dst_wins`: output second virtual index within the block's group; block k belongs to group k // 8.
All inputs are finite; a program needn't handle non-finite values.
Results may differ from a plain program's by a relative error of at most 0.0003.
Values may be sent and summed in bfloat16 or wider, within the bound.
A program may use at most 64 MiB of HBM per device.

v0:
```python
import jax
import jax.numpy as jnp
from jax import lax
from jax.sharding import PartitionSpec as P


def local(
    amplitudes,
    pp_blocks,
    src_tiles,
    src_wins,
    dst_tiles,
    dst_wins,
    hh_integrals,
    pair_gap,
    vir_energy,
    win_energy,
):
    width, npair, ncol = amplitudes.shape
    tile = pp_blocks.shape[-1]
    local_tiles = ncol // tile
    all_tiles = local_tiles * lax.axis_size("rep")
    weights = pp_blocks[0]
    in_tile = src_tiles[0]
    in_win = src_wins[0]
    out_tile = dst_tiles[0]
    out_win = dst_wins[0]
    piece = lax.all_gather(amplitudes, "int", axis=0, tiled=True)
    count = piece.shape[0]
    slabs = piece.reshape(count, npair, local_tiles, tile)
    hit_win = in_win[:, None] == jnp.arange(count, dtype=jnp.int32)[None, :]
    hit_tile = in_tile[:, None] == jnp.arange(local_tiles, dtype=jnp.int32)[None, :]
    pick = (hit_win[:, :, None] & hit_tile[:, None, :]).astype(jnp.bfloat16)
    chosen = jnp.einsum("wpst,kws->kpt", slabs, pick, preferred_element_type=jnp.float32)
    chosen = chosen.astype(jnp.bfloat16)
    product = jnp.einsum("kpt,ktu->kpu", chosen, weights, preferred_element_type=jnp.float32)
    hit_out = out_win[:, None, None] == jnp.arange(width, dtype=jnp.int32)[None, :, None]
    hit_col = out_tile[:, None, None] == jnp.arange(all_tiles, dtype=jnp.int32)[None, None, :]
    place = (hit_out & hit_col).astype(jnp.float32)
    partial_value = jnp.einsum("kpu,kbc->bpcu", product, place, precision=lax.Precision.HIGHEST)
    particle = lax.psum_scatter(
        partial_value.reshape(width, npair, all_tiles * tile),
        "rep",
        scatter_dimension=2,
        tiled=True,
    )
    own_rows = lax.dynamic_slice_in_dim(hh_integrals, lax.axis_index("amp") * npair, npair, 0)
    hole = jnp.einsum(
        "pq,bqa->bpa",
        own_rows,
        lax.all_gather(amplitudes, "amp", axis=1, tiled=True),
        preferred_element_type=jnp.float32,
    )
    denom = win_energy[:, None, None] + pair_gap[None, :, None] + vir_energy[None, None, :]
    return (particle + hole) / denom


def solution(mesh):
    placed = (
        P("int", "amp", "rep"),
        P("rep", "int", None, None),
        P("rep", "int"),
        P("rep", "int"),
        P("rep", "int"),
        P("rep", "int"),
        P(),
        P("amp"),
        P("rep"),
        P("int"),
    )
    return jax.shard_map(
        local, mesh=mesh, in_specs=placed, out_specs=P("int", "amp", "rep"), check_vma=False
    )
```

profile of v0, /device:TPU:1, one launch (start us, length us, event | category | flops | bytes accessed | tf_op | source)
XLA Modules:
  0.0 196.5 jit_solution(13614272729546214355)
XLA Ops:
  6.5 0.0 copy-start
  6.5 0.7 all-gather.3.cloned.1.call-update
  7.3 0.0 all-gather.5.cloned.1.call-start
  7.3 0.7 all-gather.5.cloned.1.call-update
  8.0 0.0 reduce-scatter.2.cloned.1.call-start
  8.1 0.7 iota_compare_fusion.3
  8.7 0.7 iota_compare_fusion
  9.4 0.7 iota_compare_fusion.1
  10.2 0.7 iota_compare_fusion.2
  10.9 0.1 and_bitcast_fusion
  11.0 63.8 %all-gather.3.cloned.1.call-done = bf16[32,128,1024]{2,1,0:T(8,128)(2,1)} async-done(((bf16[2,128,1024]{2,1,0:T(8,128)(2,1)}), bf16[32,128,1024]{2,1,0:T(8,128)(2,1)}) %all-gather.3.cloned.1.call-update) | async-done | bytes 8388624 | tf_op jit(solution)/shard_map/all_gather | solution.py:28
  74.8 8.8 %copy.16 = bf16[512,8,8,128]{3,2,1,0:T(8,128)(2,1)} copy(bf16[512,8,8,128]{3,1,2,0:T(8,128)(2,1)} %bitcast.44) | data formatting | bytes 16777216
  83.6 7.1 %fusion = bf16[8,128,128,1]{2,0,3,1:T(8,128)(2,1)S(1)} fusion(pred[8,32,8,1]{2,1,0,3:T(32,128)(4,1)S(1)} %and_bitcast_fusion, bf16[32,128,8,128]{3,2,1,0:T(8,128)(2,1)} %bitcast.45), kind=kOutput, calls=%fused_computation | convolution fusion | flops 67108864 | bytes 8652800 | tf_op jit(solution)/shard_map/wpst,kws->kpt/dot_general | solution.py:34
  90.6 0.2 fusion.6
  90.9 3.6 %convolution_bitcast_fusion = f32[2,128,32,128]{3,2,1,0:T(8,128)} fusion(f32[8,128,128]{2,1,0:T(8,128)S(1)} %fusion.6, pred[8,32]{1,0:T(8,128)(4,1)S(1)} %iota_compare_fusion.2, pred[8,2]{0,1:T(4,128)(4,1)S(1)} %iota_compare_fusion.3), kind=kOutput, calls=%fused_computation.2 | convolution fusion | flops 100663808 | bytes 4718864 | tf_op jit(solution)/shard_map/kpu,kbc->bpcu/dot_general | solution.py:40
  94.5 5.0 %reshape.136 = f32[2,128,4096]{2,1,0:T(8,128)} reshape(f32[2,128,32,128]{3,2,1,0:T(8,128)} %convolution_bitcast_fusion) | data formatting | bytes 8388608 | tf_op jit(solution)/shard_map/reshape | solution.py:42
  99.5 0.0 reduce-scatter.2.cloned.1.call-update
  99.5 0.6 copy-done.2
  100.1 0.0 copy-done.3
  100.1 0.1 broadcast_add_fusion
  100.2 31.4 %all-gather.5.cloned.1.call-done = bf16[2,1024,1024]{2,1,0:T(8,128)(2,1)} async-done(((bf16[2,128,1024]{2,1,0:T(8,128)(2,1)}), bf16[2,1024,1024]{2,1,0:T(8,128)(2,1)}) %all-gather.5.cloned.1.call-update) | async-done | bytes 4194320 | tf_op jit(solution)/shard_map/all_gather | solution.py:51
  131.6 54.1 %reduce-scatter.2.cloned.1.call-done = f32[2,128,1024]{2,1,0:T(8,128)} async-done(((f32[2,128,4096]{2,1,0:T(8,128)}), f32[2,128,1024]{2,1,0:T(8,128)}) %reduce-scatter.2.cloned.1.call-update) | async-done | bytes 1048592 | tf_op jit(solution)/shard_map/reduce_scatter | solution.py:41
  185.7 0.0 copy-done
  185.7 4.2 %fusion.3 = f32[2,128,1024]{2,1,0:T(8,128)} fusion(f32[2,128,1024]{2,1,0:T(8,128)} %reduce-scatter.2.cloned.1.call-done, bf16[2,1024,1024]{2,1,0:T(8,128)(2,1)} %all-gather.5.cloned.1.call-done, f32[1024]{0:T(1024)S(1)} %copy-done.4, f32[2,128]{1,0:T(2,128)S(1)} %broadcast_add_fusion, bf16[1024,1024]{1,0:T(8,128)(2,1)S(1)} %copy-done, s32[]{:T(128)S(6)} %select_n.3), kind=kOutput, calls=%fused_computation.5 | convolution fusion | flops 537657344 | bytes 6558724 | tf_op jit(solution)/shard_map/pq,bqa->bpa/dot_general | solution.py:48
  (7 shorter events, 0.0 us)
Async XLA Ops:
  6.5 179.2 %copy-start = (bf16[1024,1024]{1,0:T(8,128)(2,1)S(1)}, bf16[1024,1024]{1,0:T(8,128)(2,1)}, u32[]{:S(2)}) copy-start(bf16[1024,1024]{1,0:T(8,128)(2,1)} %param.16) | copy-start | bytes 6291460
  6.5 68.2 %all-gather.3.cloned.1.call-start = ((), (), s32[]{:S(2)}) async-start(), calls=%async_computation.1 | async-start | bytes 8912896 | tf_op jit(solution)/shard_map/all_gather | solution.py:28
  7.3 124.4 %all-gather.5.cloned.1.call-start = ((), (), s32[]{:S(2)}) async-start(), calls=%async_computation.3 | async-start | bytes 4718592 | tf_op jit(solution)/shard_map/all_gather | solution.py:51
  8.0 177.7 %reduce-scatter.2.cloned.1.call-start = ((), (), s32[]{:S(2)}) async-start(), calls=%async_computation.2 | async-start | bytes 5242880 | tf_op jit(solution)/shard_map/reduce_scatter | solution.py:41
  83.5 7.1 %copy-start.1 = (bf16[1,8,128,128]{3,2,1,0:T(8,128)(2,1)S(1)}, bf16[1,8,128,128]{3,2,1,0:T(8,128)(2,1)}, u32[]{:S(2)}) copy-start(bf16[1,8,128,128]{3,2,1,0:T(8,128)(2,1)} %param.11) | copy-start | bytes 786436
  99.5 0.7 copy-start.2
  99.5 0.7 copy-start.3
  99.5 86.3 %copy-start.4 = (f32[1024]{0:T(1024)S(1)}, f32[1024]{0:T(1024)}, u32[]{:S(2)}) copy-start(f32[1024]{0:T(1024)} %param.18) | copy-start | bytes 12292
Sparse Core Ops, SparseCore 0:
  9.5 65.2 all-gather.2
  76.8 54.7 all-gather.4
  134.5 51.2 reduce-scatter.1
where the time goes:
time: 197 us; the launch traced here: 196 us
  waiting for transfers between devices  151 us (77%)
  matrix products  15.2 us (8%)
  local copies, waits for them, and re-layouts  14.4 us (7%)
  between operations  13.1 us (7%)
  other arithmetic  3.01 us (2%)
    all_gather x1, waiting for transfers between devices, local(): piece = lax.all_gather(amplitudes, 'int', axis=0, tiled=True)  63.8 us
    reduce_scatter x1, waiting for transfers between devices, local(): lax.psum_scatter(partial_value.reshape(width, npair, all_tiles * tile), '...  54.1 us
    all_gather x1, waiting for transfers between devices, local(): lax.all_gather(amplitudes, 'amp', axis=1, tiled=True)  31.4 us
    unnamed x11, local copies, waits for them, and re-layouts  9.44 us
    dot_general x1, matrix products, local(): jnp.einsum('wpst,kws->kpt', slabs, pick, preferred_element_type=jnp.float32)  7.07 us
    reshape x1, local copies, waits for them, and re-layouts, local(): partial_value.reshape(width, npair, all_tiles * tile)  4.96 us
    dot_general x1, matrix products, local(): jnp.einsum('pq,bqa->bpa', own_rows, lax.all_gather(amplitudes, 'amp', axi...  4.23 us
  transfers between devices with their start and end apart: 3, of which 3 were waited for; matrix products, arithmetic and copies ran while one was open for 14% of the time, Pallas kernels for 0%

commit v1 on v0

v1 whole, which is shorter than its diff:
```python
import functools

import jax
import jax.numpy as jnp
from jax import lax
from jax.experimental import pallas as pl
from jax.experimental.pallas import tpu as pltpu
from jax.sharding import PartitionSpec as P

MESH = pl.DeviceIdType.MESH
CHUNK = 1
GAP = 5
LEVELS = 32760.0
LEAST = 1e-33


def hops(direction, chain, nz):
    return nz // 2 - ((chain + direction) % 2)


def z_order(nz, chains):
    order = []
    lists = []
    for direction in (0, 1):
        sent = {j: 0 for j in range(chains)}
        last = {j: -GAP for j in range(chains)}
        seq = []
        tick = 0
        while any(sent[j] < hops(direction, j, nz) for j in sent):
            ready = [j for j in sent if sent[j] < hops(direction, j, nz) and tick - last[j] >= GAP]
            if ready:
                j = ready[0]
                seq.append((tick, direction, j, sent[j]))
                sent[j] += 1
                last[j] = tick
            tick += 1
        lists.extend(seq)
    order = sorted(lists)
    return order


def kernel(
    ny, nz, nx, chains,
    st_ref, sw_ref, dt_ref, dw_ref, amp_ref, blk_ref, h_ref, gap_ref, vir_ref, win_ref,
    out_ref,
    tab, gap, vir, win, inv, achip, x_in, hv, ball, sall, zinj, zbuf, idxv, idxs, ysend, ssend, yrecv, srecv, yown, acc, prod,
    tab_sem, amp_sem, loc_sem, sib_sem, idx_ss, idx_rs, y1_ss, y1_rs, y2_ss, y2_rs, z_ss, z_rs, b_ss, b_rs, s_ss, s_rs,
):
    width, rows, ncol = amp_ref.shape
    tile = blk_ref.shape[-1]
    tiles = ncol // tile
    per_chip = 2 * width
    slots = blk_ref.shape[1]
    y = lax.axis_index("amp")
    i = lax.axis_index("int")
    x = lax.axis_index("rep")
    z = i // 2
    core = lax.rem(i, 2)

    def ypeer(d):
        return {"amp": lax.rem(y + (d + ny) % ny, ny)}

    def zpeer(d):
        return {"int": lax.rem(i + 2 * ((d + nz) % nz), 2 * nz)}

    def xpeer(d):
        return {"rep": lax.rem(x + (d + nx) % nx, nx)}

    sibling = {"int": i + 1 - 2 * core}
    peers = [ypeer(d) for d in range(1, ny)] + [zpeer(d) for d in range(1, nz)]
    peers += [xpeer(d) for d in range(1, nx)] + [sibling]

    def remote(src, dst, ss, rs, peer):
        return pltpu.make_async_remote_copy(
            src_ref=src, dst_ref=dst, send_sem=ss, recv_sem=rs, device_id=peer, device_id_type=MESH
        )

    def span(index, size):
        return pl.ds(pl.multiple_of(index * size, size), size)

    sends = []

    def send(copy):
        copy.start()
        sends.append(copy)

    barrier = pltpu.get_barrier_semaphore()
    for peer in peers:
        pl.semaphore_signal(barrier, inc=1, device_id=peer, device_id_type=MESH)

    own_tab = [
        pltpu.make_async_copy(ref, tab.at[n], tab_sem.at[n])
        for n, ref in enumerate((st_ref, sw_ref, dt_ref, dw_ref))
    ]
    own_en = [
        pltpu.make_async_copy(ref, to, tab_sem.at[4 + n])
        for n, (ref, to) in enumerate(((gap_ref, gap), (vir_ref, vir), (win_ref, win)))
    ]
    own_amp = [
        pltpu.make_async_copy(
            amp_ref.at[:, :, t * tile : (t + 1) * tile], achip.at[t, pl.ds(core * width, width)], amp_sem.at[t]
        )
        for t in range(tiles)
    ]
    own_h = pltpu.make_async_copy(h_ref, hv, loc_sem.at[1])
    own_blk = pltpu.make_async_copy(blk_ref.at[0], ball.at[x], loc_sem.at[2])
    own_x = [
        pltpu.make_async_copy(
            amp_ref.at[b, :, span(y, tile)], x_in.at[b, span(y, rows), :], loc_sem.at[3 + b]
        )
        for b in range(width)
    ]
    for copy in own_tab + own_x + own_amp + [own_h, own_blk] + own_en:
        copy.start()
    for copy in own_tab:
        copy.wait()
    for place in (z, nz + x):
        idxv[place] = jnp.zeros(idxv.shape[1:], jnp.int32)
        for row in range(4):
            idxv[place, row : row + 1, 0:slots] = tab[row]
    pl.semaphore_wait(barrier, len(peers))

    idx_z = [remote(idxv.at[z], idxv.at[z], idx_ss.at[d], idx_rs.at[d], zpeer(d)) for d in range(1, nz)]
    idx_x = [
        remote(idxv.at[nz + x], idxv.at[nz + x], idx_ss.at[nz + d], idx_rs.at[nz + d], xpeer(d))
        for d in range(1, nx)
    ]
    for copy in idx_z:
        send(copy)
    twin = []
    for t in range(tiles):
        part = achip.at[t, pl.ds(core * width, width)]
        twin.append(
            remote(amp_ref.at[:, :, t * tile : (t + 1) * tile], part, sib_sem.at[0, t], sib_sem.at[1, t], sibling)
        )
        send(twin[t])
    far_first = sorted(range(1, ny), key=lambda d: -min(d, ny - d))
    first = {}
    for b in range(width):
        for d in far_first:
            to = lax.rem(y + d, ny)
            first[b, d] = remote(
                amp_ref.at[b, :, span(to, tile)],
                x_in.at[b, span(y, rows), :],
                y1_ss.at[b, d],
                y1_rs.at[b, d],
                ypeer(d),
            )
            send(first[b, d])
    for copy in idx_x:
        send(copy)
    shared = [remote(blk_ref.at[0], ball.at[x], b_ss.at[d], b_rs.at[d], xpeer(d)) for d in range(1, nx)]
    for copy in shared:
        send(copy)

    for copy in idx_z:
        copy.wait_recv()
    table = pltpu.make_async_copy(idxv.at[0:nz], idxs.at[0:nz], loc_sem.at[6])
    table.start()
    table.wait()
    for t in range(tiles):
        own_amp[t].wait()
        twin[t].wait_recv()

    def slab(place, slot):
        win = idxs[place, 1, slot]
        col = idxs[place, 0, slot]
        return lax.div(win, per_chip), achip[col, lax.rem(win, per_chip)]

    moves = {}

    def z_message(direction, chain, hop):
        far = hops(direction, chain, nz)
        sign = 1 - 2 * direction
        dest = lax.rem(z + (sign * (far - hop) + nz) % nz, nz)
        if hop == 0:
            buf = zinj.at[direction, chain]
        else:
            buf = zbuf.at[direction, chain, hop - 1]
            moves[direction, chain, hop - 1].wait_recv()
        for k in range(CHUNK):
            owner, value = slab(dest, chain * CHUNK + k)
            if hop > 0:
                value = jnp.where(owner == z, value, buf[k])
            buf[k] = value
        moves[direction, chain, hop] = remote(
            buf,
            zbuf.at[direction, chain, hop],
            z_ss.at[direction, chain, hop],
            z_rs.at[direction, chain, hop],
            zpeer(sign),
        )
        send(moves[direction, chain, hop])

    spread = {}

    def z_final(chain):
        last = [hops(direction, chain, nz) for direction in (0, 1)]
        for direction in (0, 1):
            moves[direction, chain, last[direction] - 1].wait_recv()
        for k in range(CHUNK):
            slot = chain * CHUNK + k
            owner, value = slab(z, slot)
            behind = lax.rem(z - owner + nz, nz)
            up = zbuf[0, chain, last[0] - 1, k]
            down = zbuf[1, chain, last[1] - 1, k]
            value = jnp.where(owner == z, value, jnp.where(behind <= last[0], up, down))
            sall[x, slot] = value
        part = sall.at[x, pl.ds(chain * CHUNK, CHUNK)]
        for d in (list(range(2, nx)) + [1]):
            spread[chain, d] = remote(part, part, s_ss.at[chain, d], s_rs.at[chain, d], xpeer(d))
            send(spread[chain, d])

    state = {"blocks": False, "own": set(), "h": False}

    def products(chain):
        if not state["blocks"]:
            own_blk.wait()
            for copy in idx_x + shared:
                copy.wait_recv()
            more = pltpu.make_async_copy(idxv.at[nz : nz + nx], idxs.at[nz : nz + nx], loc_sem.at[5])
            more.start()
            more.wait()
            state["blocks"] = True
        keys = []
        for d in range(nx):
            origin = lax.rem(x - d + nx, nx)
            if d > 0:
                spread[chain, d].wait_recv()
            for k in range(CHUNK):
                slot = chain * CHUNK + k
                prod[d * CHUNK + k] = jnp.dot(
                    sall[origin, slot], ball[origin, slot], preferred_element_type=jnp.float32
                )
                keys.append(idxs[nz + origin, 3, slot] * (tiles * nx) + idxs[nz + origin, 2, slot] - x * tiles)

        def place(o, carry):
            b = o // tiles
            key = b * (tiles * nx) + o - b * tiles
            total = jnp.zeros((rows, tile), jnp.float32) if chain == 0 else acc[o]
            for n, found in enumerate(keys):
                total = total + prod[n] * jnp.where(found == key, 1.0, 0.0).astype(jnp.float32)
            acc[o] = total
            return carry

        lax.fori_loop(0, width * tiles, place, 0)

    def denominators():
        for copy in own_en:
            copy.wait()
        column = jnp.transpose(jnp.broadcast_to(gap[...], (rows, tile)))
        for b in range(width):
            for t in range(tiles):
                inv[b * tiles + t] = 1.0 / (win[0, b] + column + vir[t : t + 1, :])

    second = {}

    def hole(b, d):
        if b not in state["own"]:
            own_x[b].wait()
            for e in far_first:
                first[b, e].wait_recv()
            state["own"].add(b)
        if not state["h"]:
            own_h.wait()
            state["h"] = True
        to = lax.rem(y + d, ny)
        value = jnp.dot(hv[span(to, rows), :], x_in[b], preferred_element_type=jnp.float32)
        if d == 0:
            yown[b] = value
            return
        top = jnp.maximum(jnp.max(jnp.abs(value), axis=0, keepdims=True), LEAST)
        code = jnp.floor(value * (LEVELS / top) + 0.5)
        ysend[b, d] = code.astype(jnp.int32).astype(jnp.int16)
        ssend[b, d] = jnp.broadcast_to(top * (1.0 / LEVELS), ssend.shape[2:])
        second[b, d] = [
            remote(ysend.at[b, d], yrecv.at[b, d], y2_ss.at[0, b, d], y2_rs.at[0, b, d], ypeer(d)),
            remote(ssend.at[b, d], srecv.at[b, d], y2_ss.at[1, b, d], y2_rs.at[1, b, d], ypeer(d)),
        ]
        for copy in second[b, d]:
            send(copy)

    def finish(b, d):
        col = lax.rem(y - d + ny, ny)
        if d == 0:
            value = yown[b]
        else:
            for copy in second[b, d]:
                copy.wait_recv()
            value = yrecv[b, d].astype(jnp.int32).astype(jnp.float32) * srecv[b, d, 0:1, :]
        out_ref[b, :, span(col, tile)] = (acc[b * tiles + col] + value) * inv[b * tiles + col]

    step = 0.65 * CHUNK
    events = []
    ends = {}
    for n, (tick, direction, chain, hop) in enumerate(z_order(nz, chains)):
        when = 2.5 + step * tick
        events.append((when, n, functools.partial(z_message, direction, chain, hop)))
        if hop == hops(direction, chain, nz) - 1:
            ends[chain] = max(ends.get(chain, 0.0), when)
    for chain in range(chains):
        events.append((ends[chain] + step + 1.5, 1000 + chain, functools.partial(z_final, chain)))
        events.append((ends[chain] + 2 * step + 4.5, 2000 + chain, functools.partial(products, chain)))
    for b in range(width):
        for n, d in enumerate(far_first + [0]):
            events.append((7.5 + 5.3 * b + 0.5 * n, 3000 + n, functools.partial(hole, b, d)))
    events.append((5.0, 5000, denominators))
    for b in range(width):
        for n, d in enumerate([0] + far_first):
            events.append((100.0 + b, 4000 + n, functools.partial(finish, b, d)))
    for _, _, event in sorted(events, key=lambda e: e[:2]):
        event()
    for copy in sends:
        copy.wait_send()


def local(
    amplitudes,
    pp_blocks,
    src_tiles,
    src_wins,
    dst_tiles,
    dst_wins,
    hh_integrals,
    pair_gap,
    vir_energy,
    win_energy,
):
    ny = lax.axis_size("amp")
    nz = lax.axis_size("int") // 2
    nx = lax.axis_size("rep")
    width, rows, ncol = amplitudes.shape
    tile = pp_blocks.shape[-1]
    slots = pp_blocks.shape[1]
    tiles = ncol // tile
    chains = slots // CHUNK
    bf, f32, i32 = jnp.bfloat16, jnp.float32, jnp.int32
    dma = pltpu.SemaphoreType.DMA
    vmem = pl.BlockSpec(memory_space=pltpu.VMEM)
    hbm = pl.BlockSpec(memory_space=pltpu.HBM)
    return pl.pallas_call(
        functools.partial(kernel, ny, nz, nx, chains),
        out_shape=jax.ShapeDtypeStruct((width, rows, ncol), f32),
        in_specs=[hbm] * 10,
        out_specs=vmem,
        scratch_shapes=[
            pltpu.VMEM((4, 1, slots), i32),
            pltpu.VMEM((1, rows), f32),
            pltpu.VMEM((tiles, tile), f32),
            pltpu.SMEM((1, width), f32),
            pltpu.VMEM((width * tiles, rows, tile), f32),
            pltpu.VMEM((tiles, 2 * width, rows, tile), bf),
            pltpu.VMEM((width, ny * rows, tile), bf),
            pltpu.VMEM(hh_integrals.shape, bf),
            pltpu.VMEM((nx, slots, tile, tile), bf),
            pltpu.VMEM((nx, slots, rows, tile), bf),
            pltpu.VMEM((2, chains, CHUNK, rows, tile), bf),
            pltpu.VMEM((2, chains, nz // 2, CHUNK, rows, tile), bf),
            pltpu.VMEM((nz + nx, 8, 128), i32),
            pltpu.SMEM((nz + nx, 8, 128), i32),
            pltpu.VMEM((width, ny, rows, tile), jnp.int16),
            pltpu.VMEM((width, ny, 8, tile), f32),
            pltpu.VMEM((width, ny, rows, tile), jnp.int16),
            pltpu.VMEM((width, ny, 8, tile), f32),
            pltpu.VMEM((width, rows, tile), f32),
            pltpu.VMEM((width * tiles, rows, tile), f32),
            pltpu.VMEM((nx * CHUNK, rows, tile), f32),
            dma((7,)),
            dma((tiles,)),
            dma((8,)),
            dma((2, tiles)),
            dma((nz + nx,)),
            dma((nz + nx,)),
            dma((width, ny)),
            dma((width, ny)),
            dma((2, width, ny)),
            dma((2, width, ny)),
            dma((2, chains, nz // 2)),
            dma((2, chains, nz // 2)),
            dma((nx,)),
            dma((nx,)),
            dma((chains, nx)),
            dma((chains, nx)),
        ],
        compiler_params=pltpu.CompilerParams(
            collective_id=0, has_side_effects=True, vmem_limit_bytes=40 * 1024 * 1024
        ),
        cost_estimate=pl.CostEstimate(flops=700_000_000, bytes_accessed=5_000_000, transcendentals=0),
        name="ladder",
    )(
        src_tiles, src_wins, dst_tiles, dst_wins, amplitudes, pp_blocks, hh_integrals,
        pair_gap.reshape(1, rows), vir_energy.reshape(tiles, tile), win_energy.reshape(1, width),
    )


def solution(mesh):
    placed = (
        P("int", "amp", "rep"),
        P("rep", "int", None, None),
        P("rep", "int"),
        P("rep", "int"),
        P("rep", "int"),
        P("rep", "int"),
        P(),
        P("amp"),
        P("rep"),
        P("int"),
    )
    return jax.shard_map(
        local, mesh=mesh, in_specs=placed, out_specs=P("int", "amp", "rep"), check_vma=False
    )
```

time: 197 us -> 68.9 us (0.35)
  the two profiles are of different devices: /device:TPU:1 before, /device:TPU:8 now
where the time goes in v1:
time: 68.9 us; the launch traced here: 68.5 us
  Pallas kernels  59.4 us (86%)
  local copies, waits for them, and re-layouts  9.17 us (13%)
    pallas_call x1, Pallas kernels, local(): pl.pallas_call(functools.partial(kernel, ny, nz, nx, chains), out_shape=j...  59.4 us
    unnamed x21, local copies, waits for them, and re-layouts  9.17 us

profile of v1, /device:TPU:8, one launch (start us, length us, event | category | flops | bytes accessed | tf_op | source)
XLA Modules:
  0.0 68.5 jit_solution(9902843266036133570)
XLA Ops:
  0.0 0.0 copy-start
  0.0 1.6 %copy-done = bf16[1024,1024]{1,0:T(8,128)(2,1)S(1)} copy-done((bf16[1024,1024]{1,0:T(8,128)(2,1)S(1)}, bf16[1024,1024]{1,0:T(8,128)(2,1)}, u32[]{:S(2)}) %copy-start) | copy-done | bytes 2097176
  1.6 0.0 copy-start.1
  1.6 1.0 %copy-done.1 = bf16[2,128,1024]{2,1,0:T(8,128)(2,1)S(1)} copy-done((bf16[2,128,1024]{2,1,0:T(8,128)(2,1)S(1)}, bf16[2,128,1024]{2,1,0:T(8,128)(2,1)}, u32[]{:S(2)}) %copy-start.1) | copy-done | bytes 524312
  2.6 0.0 copy-start.2
  2.6 0.9 %copy-done.2 = bf16[1,8,128,128]{3,2,1,0:T(8,128)(2,1)S(1)} copy-done((bf16[1,8,128,128]{3,2,1,0:T(8,128)(2,1)S(1)}, bf16[1,8,128,128]{3,2,1,0:T(8,128)(2,1)}, u32[]{:S(2)}) %copy-start.2) | copy-done | bytes 262168
  3.6 0.0 copy-start.3
  3.6 0.7 copy-done.3
  4.3 0.0 copy-start.4
  4.3 0.7 copy-done.4
  4.9 0.0 copy-start.5
  4.9 0.7 copy-done.5
  5.6 0.0 copy-start.6
  5.6 0.7 copy-done.6
  6.2 0.0 copy-start.7
  6.2 0.7 copy-done.7
  6.9 0.0 copy-start.8
  6.9 0.7 copy-done.8
  7.6 0.0 copy-start.9
  7.6 0.7 copy-done.9
  8.2 59.4 %ladder.1 = f32[2,128,1024]{2,1,0:T(8,128)S(1)} custom-call(s32[1,8]{1,0:T(1,128)S(1)} %copy-done.4, s32[1,8]{1,0:T(1,128)S(1)} %copy-done.5, s32[1,8]{1,0:T(1,128)S(1)} %copy-done.6, s32[1,8]{1,0:T(1,128)S(1)} %copy-done.7, bf16[2,128,1024]{2,1,0:T(8,128)(2,1)S(1)} %copy-done.1, bf16[1,8,128,128]{3,2,1,0:T(8,128)(2,1)S(1)} %copy-done.2, ...), custom_call_target="tpu_custom_call" | custom-call | flops 700000000 | bytes 5000000 | tf_op jit(solution)/shard_map/ladder/pallas_call | solution.py:341
  67.6 1.0 %copy.12 = f32[2,128,1024]{2,1,0:T(8,128)} copy(f32[2,128,1024]{2,1,0:T(8,128)S(1)} %ladder.1) | data formatting | bytes 2097152
Async XLA Ops:
  0.0 1.6 %copy-start = (bf16[1024,1024]{1,0:T(8,128)(2,1)S(1)}, bf16[1024,1024]{1,0:T(8,128)(2,1)}, u32[]{:S(2)}) copy-start(bf16[1024,1024]{1,0:T(8,128)(2,1)} %h_ref.1) | copy-start | bytes 6291460
  1.6 1.0 %copy-start.1 = (bf16[2,128,1024]{2,1,0:T(8,128)(2,1)S(1)}, bf16[2,128,1024]{2,1,0:T(8,128)(2,1)}, u32[]{:S(2)}) copy-start(bf16[2,128,1024]{2,1,0:T(8,128)(2,1)} %amp_ref.1) | copy-start | bytes 1572868
  2.6 0.9 %copy-start.2 = (bf16[1,8,128,128]{3,2,1,0:T(8,128)(2,1)S(1)}, bf16[1,8,128,128]{3,2,1,0:T(8,128)(2,1)}, u32[]{:S(2)}) copy-start(bf16[1,8,128,128]{3,2,1,0:T(8,128)(2,1)} %blk_ref.1) | copy-start | bytes 786436
  3.6 0.7 %copy-start.3 = (f32[1024]{0:T(1024)S(1)}, f32[1024]{0:T(1024)}, u32[]{:S(2)}) copy-start(f32[1024]{0:T(1024)} %param.18) | copy-start | bytes 12292
  4.3 0.7 copy-start.4
  4.9 0.7 copy-start.5
  5.6 0.7 copy-start.6
  6.2 0.7 copy-start.7
  6.9 0.7 copy-start.8
  7.6 0.7 copy-start.9

commit v2 on v1

--- a/solution.py
+++ b/solution.py
@@ -9,33 +9,58 @@
 
 MESH = pl.DeviceIdType.MESH
 CHUNK = 1
-GAP = 5
 LEVELS = 32760.0
 LEAST = 1e-33
+SLAB, DUE, APART, HOP, DELAY, SHARE, SHARE_DELAY = 0.65, 9.75, 1.95, 3.9, 1.5, 1.3, 1.8
+START, COST_Z, COST_F, COST_P, COST_H = 5.0, 0.12, 0.2, 0.7, 0.45
 
 
 def hops(direction, chain, nz):
     return nz // 2 - ((chain + direction) % 2)
 
 
-def z_order(nz, chains):
-    order = []
-    lists = []
-    for direction in (0, 1):
-        sent = {j: 0 for j in range(chains)}
-        last = {j: -GAP for j in range(chains)}
-        seq = []
-        tick = 0
-        while any(sent[j] < hops(direction, j, nz) for j in sent):
-            ready = [j for j in sent if sent[j] < hops(direction, j, nz) and tick - last[j] >= GAP]
-            if ready:
-                j = ready[0]
-                seq.append((tick, direction, j, sent[j]))
-                sent[j] += 1
-                last[j] = tick
-            tick += 1
-        lists.extend(seq)
-    order = sorted(lists)
+def plan(nz, chains, width, ny):
+    slab, share = SLAB * CHUNK, SHARE * CHUNK
+    todo = {}
+    for j in range(chains):
+        due = DUE + APART * j * CHUNK
+        for d in (0, 1):
+            for h in range(hops(d, j, nz)):
+                todo["z", d, j, h] = due - (hops(d, j, nz) - 1 - h) * HOP
+        todo["f", j] = due + DELAY
+        todo["p", j] = due + DELAY + 6.0
+    landed = [2.0 + (b + 1) * ny * SLAB + DELAY for b in range(width)]
+    for b in range(width):
+        for n in range(ny):
+            todo["h", b, n] = landed[b] + n * SLAB
+    now, zfree, xfree, arrive, order = 0.0, [0.0, 0.0], 0.0, {}, []
+
+    def ready(k):
+        if k[0] == "z":
+            return START if k[3] == 0 else arrive.get(("z", k[1], k[2], k[3] - 1), 1e9)
+        if k[0] == "f":
+            return max(arrive.get(("z", d, k[1], hops(d, k[1], nz) - 1), 1e9) for d in (0, 1))
+        return landed[k[1]] if k[0] == "h" else arrive.get(k, 1e9)
+
+    while todo:
+        when = {k: ready(k) for k in todo}
+        open_now = [k for k in todo if when[k] <= now]
+        if not open_now:
+            now = min(when.values())
+            continue
+        k = min(open_now, key=lambda k: (todo[k], k))
+        del todo[k]
+        order.append(k)
+        if k[0] == "z":
+            now += COST_Z
+            zfree[k[1]] = max(now, zfree[k[1]]) + slab
+            arrive[k] = zfree[k[1]] + DELAY
+        elif k[0] == "f":
+            now += COST_F
+            xfree = max(now, xfree) + share
+            arrive["p", k[1]] = xfree + SHARE_DELAY
+        else:
+            now += COST_P if k[0] == "p" else COST_H
     return order
 
 
@@ -43,7 +68,7 @@
     ny, nz, nx, chains,
     st_ref, sw_ref, dt_ref, dw_ref, amp_ref, blk_ref, h_ref, gap_ref, vir_ref, win_ref,
     out_ref,
-    tab, gap, vir, win, inv, achip, x_in, hv, ball, sall, zinj, zbuf, idxv, idxs, ysend, ssend, yrecv, srecv, yown, acc, prod,
+    gap, vir, win, inv, achip, x_in, hv, ball, sall, zinj, zbuf, idxs, ysend, ssend, yrecv, srecv, yown, acc, prod,
     tab_sem, amp_sem, loc_sem, sib_sem, idx_ss, idx_rs, y1_ss, y1_rs, y2_ss, y2_rs, z_ss, z_rs, b_ss, b_rs, s_ss, s_rs,
 ):
     width, rows, ncol = amp_ref.shape
@@ -88,9 +113,10 @@
     for peer in peers:
         pl.semaphore_signal(barrier, inc=1, device_id=peer, device_id_type=MESH)
 
+    lists = (st_ref, sw_ref, dt_ref, dw_ref)
     own_tab = [
-        pltpu.make_async_copy(ref, tab.at[n], tab_sem.at[n])
-        for n, ref in enumerate((st_ref, sw_ref, dt_ref, dw_ref))
+        pltpu.make_async_copy(ref, idxs.at[place, n % 2], tab_sem.at[n])
+        for n, (ref, place) in enumerate(zip(lists, (z, z, nz + x, nz + x)))
     ]
     own_en = [
         pltpu.make_async_copy(ref, to, tab_sem.at[4 + n])
@@ -112,18 +138,16 @@
     ]
     for copy in own_tab + own_x + own_amp + [own_h, own_blk] + own_en:
         copy.start()
-    for copy in own_tab:
-        copy.wait()
-    for place in (z, nz + x):
-        idxv[place] = jnp.zeros(idxv.shape[1:], jnp.int32)
-        for row in range(4):
-            idxv[place, row : row + 1, 0:slots] = tab[row]
     pl.semaphore_wait(barrier, len(peers))
 
-    idx_z = [remote(idxv.at[z], idxv.at[z], idx_ss.at[d], idx_rs.at[d], zpeer(d)) for d in range(1, nz)]
+    far_z = sorted(range(1, nz), key=lambda d: -min(d, nz - d))
+    idx_z = [
+        remote(lists[n], idxs.at[z, n], idx_ss.at[n, d], idx_rs.at[n, d], zpeer(d)) for d in far_z for n in (0, 1)
+    ]
     idx_x = [
-        remote(idxv.at[nz + x], idxv.at[nz + x], idx_ss.at[nz + d], idx_rs.at[nz + d], xpeer(d))
+        remote(lists[2 + n], idxs.at[nz + x, n], idx_ss.at[n, nz + d], idx_rs.at[n, nz + d], xpeer(d))
         for d in range(1, nx)
+        for n in (0, 1)
     ]
     for copy in idx_z:
         send(copy)
@@ -155,16 +179,15 @@
 
     for copy in idx_z:
         copy.wait_recv()
-    table = pltpu.make_async_copy(idxv.at[0:nz], idxs.at[0:nz], loc_sem.at[6])
-    table.start()
-    table.wait()
+    for copy in own_tab:
+        copy.wait()
     for t in range(tiles):
         own_amp[t].wait()
         twin[t].wait_recv()
 
     def slab(place, slot):
-        win = idxs[place, 1, slot]
-        col = idxs[place, 0, slot]
+        win = idxs[place, 1, 0, slot]
+        col = idxs[place, 0, 0, slot]
         return lax.div(win, per_chip), achip[col, lax.rem(win, per_chip)]
 
     moves = {}
@@ -214,13 +237,11 @@
     state = {"blocks": False, "own": set(), "h": False}
 
     def products(chain):
+        fresh = not state["blocks"]
         if not state["blocks"]:
             own_blk.wait()
             for copy in idx_x + shared:
                 copy.wait_recv()
-            more = pltpu.make_async_copy(idxv.at[nz : nz + nx], idxs.at[nz : nz + nx], loc_sem.at[5])
-            more.start()
-            more.wait()
             state["blocks"] = True
         keys = []
         for d in range(nx):
@@ -232,12 +253,12 @@
                 prod[d * CHUNK + k] = jnp.dot(
                     sall[origin, slot], ball[origin, slot], preferred_element_type=jnp.float32
                 )
-                keys.append(idxs[nz + origin, 3, slot] * (tiles * nx) + idxs[nz + origin, 2, slot] - x * tiles)
+                keys.append(idxs[nz + origin, 1, 0, slot] * (tiles * nx) + idxs[nz + origin, 0, 0, slot] - x * tiles)
 
         def place(o, carry):
             b = o // tiles
             key = b * (tiles * nx) + o - b * tiles
-            total = jnp.zeros((rows, tile), jnp.float32) if chain == 0 else acc[o]
+            total = jnp.zeros((rows, tile), jnp.float32) if fresh else acc[o]
             for n, found in enumerate(keys):
                 total = total + prod[n] * jnp.where(found == key, 1.0, 0.0).astype(jnp.float32)
             acc[o] = total
@@ -290,26 +311,14 @@
             value = yrecv[b, d].astype(jnp.int32).astype(jnp.float32) * srecv[b, d, 0:1, :]
         out_ref[b, :, span(col, tile)] = (acc[b * tiles + col] + value) * inv[b * tiles + col]
 
-    step = 0.65 * CHUNK
-    events = []
-    ends = {}
-    for n, (tick, direction, chain, hop) in enumerate(z_order(nz, chains)):
-        when = 2.5 + step * tick
-        events.append((when, n, functools.partial(z_message, direction, chain, hop)))
-        if hop == hops(direction, chain, nz) - 1:
-            ends[chain] = max(ends.get(chain, 0.0), when)
-    for chain in range(chains):
-        events.append((ends[chain] + step + 1.5, 1000 + chain, functools.partial(z_final, chain)))
-        events.append((ends[chain] + 2 * step + 4.5, 2000 + chain, functools.partial(products, chain)))
+    runs = {"z": z_message, "f": z_final, "p": products, "h": lambda b, n: hole(b, (far_first + [0])[n])}
+    for n, (kind, *place) in enumerate(plan(nz, chains, width, ny)):
+        runs[kind](*place)
+        if n == 2 * chains:
+            denominators()
     for b in range(width):
-        for n, d in enumerate(far_first + [0]):
-            events.append((7.5 + 5.3 * b + 0.5 * n, 3000 + n, functools.partial(hole, b, d)))
-    events.append((5.0, 5000, denominators))
-    for b in range(width):
-        for n, d in enumerate([0] + far_first):
-            events.append((100.0 + b, 4000 + n, functools.partial(finish, b, d)))
-    for _, _, event in sorted(events, key=lambda e: e[:2]):
-        event()
+        for d in [0] + far_first:
+            finish(b, d)
     for copy in sends:
         copy.wait_send()
 
@@ -344,7 +353,6 @@
         in_specs=[hbm] * 10,
         out_specs=vmem,
         scratch_shapes=[
-            pltpu.VMEM((4, 1, slots), i32),
             pltpu.VMEM((1, rows), f32),
             pltpu.VMEM((tiles, tile), f32),
             pltpu.SMEM((1, width), f32),
@@ -356,8 +364,7 @@
             pltpu.VMEM((nx, slots, rows, tile), bf),
             pltpu.VMEM((2, chains, CHUNK, rows, tile), bf),
             pltpu.VMEM((2, chains, nz // 2, CHUNK, rows, tile), bf),
-            pltpu.VMEM((nz + nx, 8, 128), i32),
-            pltpu.SMEM((nz + nx, 8, 128), i32),
+            pltpu.SMEM((nz + nx, 2, 1, slots), i32),
             pltpu.VMEM((width, ny, rows, tile), jnp.int16),
             pltpu.VMEM((width, ny, 8, tile), f32),
             pltpu.VMEM((width, ny, rows, tile), jnp.int16),
@@ -369,8 +376,8 @@
             dma((tiles,)),
             dma((8,)),
             dma((2, tiles)),
-            dma((nz + nx,)),
-            dma((nz + nx,)),
+            dma((2, nz + nx)),
+            dma((2, nz + nx)),
             dma((width, ny)),
             dma((width, ny)),
             dma((2, width, ny)),
@@ -383,7 +390,7 @@
             dma((chains, nx)),
         ],
         compiler_params=pltpu.CompilerParams(
-            collective_id=0, has_side_effects=True, vmem_limit_bytes=40 * 1024 * 1024
+            collective_id=0, has_side_effects=True, vmem_limit_bytes=60 * 1024 * 1024
         ),
         cost_estimate=pl.CostEstimate(flops=700_000_000, bytes_accessed=5_000_000, transcendentals=0),
         name="ladder",

time: 68.9 us -> 57.1 us (0.83)
  the two profiles are of different devices: /device:TPU:8 before, /device:TPU:2 now
where the time goes in v2:
time: 57.1 us; the launch traced here: 56.9 us
  Pallas kernels  54.6 us (96%)
  local copies, waits for them, and re-layouts  2.31 us (4%)
    pallas_call x1, Pallas kernels, local(): pl.pallas_call(functools.partial(kernel, ny, nz, nx, chains), out_shape=j...  54.6 us
    unnamed x1, local copies, waits for them, and re-layouts  2.31 us

profile of v2, /device:TPU:2, one launch (start us, length us, event | category | flops | bytes accessed | tf_op | source)
XLA Modules:
  0.0 56.9 jit_solution(14342065750889698824)
XLA Ops:
  0.0 54.6 %ladder.1 = f32[2,128,1024]{2,1,0:T(8,128)} custom-call(s32[1,8]{1,0:T(1,128)} %st_ref.1, s32[1,8]{1,0:T(1,128)} %sw_ref.1, s32[1,8]{1,0:T(1,128)} %dt_ref.1, s32[1,8]{1,0:T(1,128)} %dw_ref.1, bf16[2,128,1024]{2,1,0:T(8,128)(2,1)} %amp_ref.1, bf16[1,8,128,128]{3,2,1,0:T(8,128)(2,1)} %blk_ref.1, bf16[1024,1024]{1,0:T(8,128)(2,1)} %h_ref.1, f32[1,128]{1,0:T(1,128)} %bitcast.4, ...), custom_call_target="tpu_custom_call" | custom-call | flops 700000000 | bytes 5000000 | tf_op jit(solution)/shard_map/ladder/pallas_call | solution.py:350
  54.6 2.3 %copy.12 = f32[2,128,1024]{2,1,0:T(8,128)} copy(f32[2,128,1024]{2,1,0:T(8,128)} %ladder.1) | data formatting | bytes 2097152

commit v3 on v2

v3 whole, which is shorter than its diff:
```python
import functools

import jax
import jax.numpy as jnp
from jax import lax
from jax.experimental import pallas as pl
from jax.experimental.pallas import tpu as pltpu
from jax.sharding import PartitionSpec as P

MESH = pl.DeviceIdType.MESH
CHUNK = 1
LEVELS = 32760.0
LEAST = 1e-33
SLAB, DUE, APART, DELAY = 0.66, 6.0, 0.6, 2.3
START, COST_Z, COST_F, COST_H = 5.0, 0.12, 0.2, 0.45
POWER = 0.85
WINDOW = 4


def hops(direction, chain, nz):
    return nz // 2 - ((chain + direction) % 2)


def plan(nz, chains, width, ny):
    slab = SLAB * CHUNK
    todo = {}
    for j in range(chains):
        due = DUE + APART * j * CHUNK
        for d in (0, 1):
            far = hops(d, j, nz)
            for h in range(far):
                todo["z", d, j, h] = START + due * (2 * (h + 1 + nz // 2 - far) / nz) ** POWER
        todo["f", j] = START + due + DELAY
    landed = [2.0 + (b + 1) * ny * SLAB + DELAY for b in range(width)]
    for b in range(width):
        for n in range(ny):
            todo["h", b, n] = landed[b] + n * SLAB
    now, zfree, arrive, order = 0.0, [0.0, 0.0], {}, []

    def ready(k):
        if k[0] == "z":
            here = START if k[3] == 0 else arrive.get(("z", k[1], k[2], k[3] - 1), 1e9)
            return max(here, zfree[k[1]] - slab)
        if k[0] == "f":
            return max(arrive.get(("z", d, k[1], hops(d, k[1], nz) - 1), 1e9) for d in (0, 1))
        return landed[k[1]]

    while todo:
        when = {k: ready(k) for k in todo}
        open_now = [k for k in todo if when[k] <= now]
        if not open_now:
            now = min(when.values())
            continue
        k = min(open_now, key=lambda k: (todo[k], k))
        del todo[k]
        order.append(k)
        if k[0] == "z":
            now += COST_Z
            zfree[k[1]] = max(now, zfree[k[1]]) + slab
            arrive[k] = zfree[k[1]] + DELAY
        elif k[0] == "f":
            now += COST_F
        else:
            now += COST_H
    return order


def kernel(
    ny, nz, nx, chains,
    st_ref, sw_ref, dt_ref, dw_ref, amp_ref, blk_ref, h_ref,
    s_out, b_out, y_out, r_out, i_out,
    achip, x_in, hv, sall, zinj, zbuf, idxs, ysend, ssend,
    tab_sem, amp_sem, loc_sem, own_sem, sib_sem, idx_ss, idx_rs, y1_ss, y1_rs, y2_ss, y2_rs, z_ss, z_rs, b_ss, b_rs, s_ss, s_rs,
):
    width, rows, ncol = amp_ref.shape
    tile = blk_ref.shape[-1]
    tiles = ncol // tile
    per_chip = 2 * width
    slots = blk_ref.shape[1]
    y = lax.axis_index("amp")
    i = lax.axis_index("int")
    x = lax.axis_index("rep")
    z = i // 2
    core = lax.rem(i, 2)

    def ypeer(d):
        return {"amp": lax.rem(y + (d + ny) % ny, ny)}

    def zpeer(d):
        return {"int": lax.rem(i + 2 * ((d + nz) % nz), 2 * nz)}

    def xpeer(d):
        return {"rep": lax.rem(x + (d + nx) % nx, nx)}

    sibling = {"int": i + 1 - 2 * core}
    peers = [ypeer(d) for d in range(1, ny)] + [zpeer(d) for d in range(1, nz)]
    peers += [xpeer(d) for d in range(1, nx)] + [sibling]

    def remote(src, dst, ss, rs, peer):
        return pltpu.make_async_remote_copy(
            src_ref=src, dst_ref=dst, send_sem=ss, recv_sem=rs, device_id=peer, device_id_type=MESH
        )

    def span(index, size):
        return pl.ds(pl.multiple_of(index * size, size), size)

    sends = []

    kept = []

    def keep(copy):
        copy.start()
        kept.append(copy)

    def send(copy):
        copy.start()
        sends.append(copy)

    barrier = pltpu.get_barrier_semaphore()
    for peer in peers:
        pl.semaphore_signal(barrier, inc=1, device_id=peer, device_id_type=MESH)

    lists = (st_ref, sw_ref, dt_ref, dw_ref)
    own_tab = [
        pltpu.make_async_copy(ref, to, tab_sem.at[n])
        for n, (ref, to) in enumerate(zip(lists, (idxs.at[z, 0], idxs.at[z, 1], i_out.at[x, 0], i_out.at[x, 1])))
    ]
    own_amp = [
        pltpu.make_async_copy(
            amp_ref.at[:, :, t * tile : (t + 1) * tile], achip.at[t, pl.ds(core * width, width)], amp_sem.at[t]
        )
        for t in range(tiles)
    ]
    own_h = pltpu.make_async_copy(h_ref, hv, loc_sem.at[1])
    own_blk = pltpu.make_async_copy(blk_ref.at[0], b_out.at[x], loc_sem.at[2])
    own_x = [
        pltpu.make_async_copy(
            amp_ref.at[b, :, span(y, tile)], x_in.at[b, span(y, rows), :], loc_sem.at[3 + b]
        )
        for b in range(width)
    ]
    for copy in own_tab + own_x + own_amp + [own_h, own_blk]:
        copy.start()
    pl.semaphore_wait(barrier, len(peers))

    far_z = sorted(range(1, nz), key=lambda d: -min(d, nz - d))
    idx_z = [
        remote(lists[n], idxs.at[z, n], idx_ss.at[n, d], idx_rs.at[n, d], zpeer(d)) for d in far_z for n in (0, 1)
    ]
    idx_x = [
        remote(lists[2 + n], i_out.at[x, n], idx_ss.at[n, nz + d], idx_rs.at[n, nz + d], xpeer(d))
        for d in range(1, nx)
        for n in (0, 1)
    ]
    for copy in idx_z:
        send(copy)
    twin = []
    for t in range(tiles):
        part = achip.at[t, pl.ds(core * width, width)]
        twin.append(
            remote(amp_ref.at[:, :, t * tile : (t + 1) * tile], part, sib_sem.at[0, t], sib_sem.at[1, t], sibling)
        )
        send(twin[t])
    far_first = sorted(range(1, ny), key=lambda d: -min(d, ny - d))
    first = {}
    for b in range(width):
        for d in far_first:
            to = lax.rem(y + d, ny)
            first[b, d] = remote(
                amp_ref.at[b, :, span(to, tile)],
                x_in.at[b, span(y, rows), :],
                y1_ss.at[b, d],
                y1_rs.at[b, d],
                ypeer(d),
            )
            send(first[b, d])
    for copy in idx_x:
        send(copy)
    shared = [remote(blk_ref.at[0], b_out.at[x], b_ss.at[d], b_rs.at[d], xpeer(d)) for d in range(1, nx)]
    for copy in shared:
        send(copy)

    for copy in idx_z:
        copy.wait_recv()
    for copy in own_tab[:2]:
        copy.wait()
    for t in range(tiles):
        own_amp[t].wait()
        twin[t].wait_recv()

    def slab(place, slot):
        win = idxs[place, 1, 0, slot]
        col = idxs[place, 0, 0, slot]
        return lax.div(win, per_chip), achip[col, lax.rem(win, per_chip)]

    moves = {}
    flying = [[], []]

    def z_message(direction, chain, hop):
        far = hops(direction, chain, nz)
        sign = 1 - 2 * direction
        dest = lax.rem(z + (sign * (far - hop) + nz) % nz, nz)
        if hop == 0:
            buf = zinj.at[direction, chain]
        else:
            buf = zbuf.at[direction, chain, hop - 1]
            moves[direction, chain, hop - 1].wait_recv()
        if len(flying[direction]) == WINDOW:
            flying[direction].pop(0).wait_send()
        for k in range(CHUNK):
            owner, value = slab(dest, chain * CHUNK + k)
            if hop > 0:
                value = jnp.where(owner == z, value, buf[k])
            buf[k] = value
        moves[direction, chain, hop] = remote(
            buf,
            zbuf.at[direction, chain, hop],
            z_ss.at[direction, chain, hop],
            z_rs.at[direction, chain, hop],
            zpeer(sign),
        )
        flying[direction].append(moves[direction, chain, hop])
        flying[direction][-1].start()

    spread = {}

    def z_final(chain):
        last = [hops(direction, chain, nz) for direction in (0, 1)]
        for direction in (0, 1):
            moves[direction, chain, last[direction] - 1].wait_recv()
        for k in range(CHUNK):
            slot = chain * CHUNK + k
            owner, value = slab(z, slot)
            behind = lax.rem(z - owner + nz, nz)
            up = zbuf[0, chain, last[0] - 1, k]
            down = zbuf[1, chain, last[1] - 1, k]
            value = jnp.where(owner == z, value, jnp.where(behind <= last[0], up, down))
            sall[slot] = value
        part = sall.at[pl.ds(chain * CHUNK, CHUNK)]
        to = s_out.at[x, pl.ds(chain * CHUNK, CHUNK)]
        for d in (list(range(2, nx)) + [1]):
            spread[chain, d] = remote(part, to, s_ss.at[chain, d], s_rs.at[chain, d], xpeer(d))
            send(spread[chain, d])
        keep(pltpu.make_async_copy(part, to, own_sem.at[chain]))

    state = {"own": set(), "h": False}

    second = {}

    def hole(b, d):
        if b not in state["own"]:
            own_x[b].wait()
            for e in far_first:
                first[b, e].wait_recv()
            state["own"].add(b)
        if not state["h"]:
            own_h.wait()
            state["h"] = True
        to = lax.rem(y + d, ny)
        value = jnp.dot(hv[span(to, rows), :], x_in[b], preferred_element_type=jnp.float32)
        top = jnp.maximum(jnp.max(jnp.abs(value), axis=0, keepdims=True), LEAST)
        code = jnp.floor(value * (LEVELS / top) + 0.5)
        ysend[b, d] = code.astype(jnp.int32).astype(jnp.int16)
        ssend[b, d] = jnp.broadcast_to(top * (1.0 / LEVELS), ssend.shape[2:])
        pairs = ((ysend.at[b, d], y_out.at[b, y]), (ssend.at[b, d], r_out.at[b, y]))
        if d == 0:
            for n, (here, there) in enumerate(pairs):
                keep(pltpu.make_async_copy(here, there, own_sem.at[chains + 2 * b + n]))
            return
        second[b, d] = [
            remote(here, there, y2_ss.at[n, b, d], y2_rs.at[n, b, d], ypeer(d))
            for n, (here, there) in enumerate(pairs)
        ]
        for copy in second[b, d]:
            send(copy)

    runs = {"z": z_message, "f": z_final, "h": lambda b, n: hole(b, (far_first + [0])[n])}
    for kind, *place in plan(nz, chains, width, ny):
        runs[kind](*place)
    own_blk.wait()
    for copy in own_tab[2:] + kept:
        copy.wait()
    for copy in idx_x + shared + list(spread.values()) + [copy for pair in second.values() for copy in pair]:
        copy.wait_recv()
    for copy in sends + flying[0] + flying[1]:
        copy.wait_send()


def finish(idx, win, s_ref, b_ref, y_ref, r_ref, gap_ref, vir_ref, out_ref, s, b, y, r, gap, vir, acc, out, sem):
    origins, slots, rows, tile = s.shape
    width, tiles = y.shape[:2]
    x = lax.axis_index("rep")
    first = [
        pltpu.make_async_copy(here, there, sem.at[n])
        for n, (here, there) in enumerate(((gap_ref, gap), (vir_ref, vir), (y_ref, y), (r_ref, r)))
    ]
    blocks = [
        [
            pltpu.make_async_copy(s_ref.at[o], s.at[o], sem.at[4 + 2 * o]),
            pltpu.make_async_copy(b_ref.at[o], b.at[o], sem.at[5 + 2 * o]),
        ]
        for o in range(origins)
    ]
    for copy in first + [copy for pair in blocks for copy in pair]:
        copy.start()
    for o in range(width * tiles + 1):
        acc[o] = jnp.zeros((rows, tile), jnp.float32)
    for o in range(origins):
        for copy in blocks[o]:
            copy.wait()
        for k in range(slots):
            place = idx[o, 1, 0, k] * tiles + idx[o, 0, 0, k] - x * tiles
            inside = (idx[o, 0, 0, k] >= x * tiles) & (idx[o, 0, 0, k] < (x + 1) * tiles)
            place = jnp.where(inside, place, width * tiles)
            acc[place] += jnp.dot(s[o, k], b[o, k], preferred_element_type=jnp.float32)
    for copy in first:
        copy.wait()
    column = jnp.transpose(jnp.broadcast_to(gap[...], (rows, tile)))
    done = []
    for n in range(width):
        for t in range(tiles):
            value = y[n, t].astype(jnp.int32).astype(jnp.float32) * r[n, t, 0:1, :] + acc[n * tiles + t]
            out[n, :, t * tile : (t + 1) * tile] = value / (win[0, n] + column + vir[t : t + 1, :])
        done.append(pltpu.make_async_copy(out.at[n], out_ref.at[n], sem.at[4 + 2 * origins + n]))
        done[n].start()
    for copy in done:
        copy.wait()


def local(
    amplitudes,
    pp_blocks,
    src_tiles,
    src_wins,
    dst_tiles,
    dst_wins,
    hh_integrals,
    pair_gap,
    vir_energy,
    win_energy,
):
    ny = lax.axis_size("amp")
    nz = lax.axis_size("int") // 2
    nx = lax.axis_size("rep")
    width, rows, ncol = amplitudes.shape
    tile = pp_blocks.shape[-1]
    slots = pp_blocks.shape[1]
    tiles = ncol // tile
    chains = slots // CHUNK
    bf, f32, i32 = jnp.bfloat16, jnp.float32, jnp.int32
    dma = pltpu.SemaphoreType.DMA
    hbm = pl.BlockSpec(memory_space=pltpu.HBM)
    smem = pl.BlockSpec(memory_space=pltpu.SMEM)
    slabs, blocks, codes, scales, places = pl.pallas_call(
        functools.partial(kernel, ny, nz, nx, chains),
        out_shape=[
            jax.ShapeDtypeStruct((nx, slots, rows, tile), bf),
            jax.ShapeDtypeStruct((nx, slots, tile, tile), bf),
            jax.ShapeDtypeStruct((width, ny, rows, tile), jnp.int16),
            jax.ShapeDtypeStruct((width, ny, 8, tile), f32),
            jax.ShapeDtypeStruct((nx, 2, 1, slots), i32),
        ],
        in_specs=[hbm] * 7,
        out_specs=[hbm] * 5,
        scratch_shapes=[
            pltpu.VMEM((tiles, 2 * width, rows, tile), bf),
            pltpu.VMEM((width, ny * rows, tile), bf),
            pltpu.VMEM(hh_integrals.shape, bf),
            pltpu.VMEM((slots, rows, tile), bf),
            pltpu.VMEM((2, chains, CHUNK, rows, tile), bf),
            pltpu.VMEM((2, chains, nz // 2, CHUNK, rows, tile), bf),
            pltpu.SMEM((nz, 2, 1, slots), i32),
            pltpu.VMEM((width, ny, rows, tile), jnp.int16),
            pltpu.VMEM((width, ny, 8, tile), f32),
            dma((4,)),
            dma((tiles,)),
            dma((8,)),
            dma((chains + 2 * width,)),
            dma((2, tiles)),
            dma((2, nz + nx)),
            dma((2, nz + nx)),
            dma((width, ny)),
            dma((width, ny)),
            dma((2, width, ny)),
            dma((2, width, ny)),
            dma((2, chains, nz // 2)),
            dma((2, chains, nz // 2)),
            dma((nx,)),
            dma((nx,)),
            dma((chains, nx)),
            dma((chains, nx)),
        ],
        compiler_params=pltpu.CompilerParams(
            collective_id=0, has_side_effects=True, vmem_limit_bytes=60 * 1024 * 1024
        ),
        cost_estimate=pl.CostEstimate(flops=700_000_000, bytes_accessed=5_000_000, transcendentals=0),
        name="ladder",
    )(src_tiles, src_wins, dst_tiles, dst_wins, amplitudes, pp_blocks, hh_integrals)
    return pl.pallas_call(
        finish,
        out_shape=jax.ShapeDtypeStruct((width, rows, ncol), f32),
        in_specs=[smem, smem] + [hbm] * 6,
        out_specs=hbm,
        scratch_shapes=[
            pltpu.VMEM(slabs.shape, bf),
            pltpu.VMEM(blocks.shape, bf),
            pltpu.VMEM(codes.shape, jnp.int16),
            pltpu.VMEM(scales.shape, f32),
            pltpu.VMEM((1, rows), f32),
            pltpu.VMEM((tiles, tile), f32),
            pltpu.VMEM((width * tiles + 1, rows, tile), f32),
            pltpu.VMEM((width, rows, ncol), f32),
            dma((4 + 2 * nx + width,)),
        ],
        compiler_params=pltpu.CompilerParams(vmem_limit_bytes=60 * 1024 * 1024),
        cost_estimate=pl.CostEstimate(flops=140_000_000, bytes_accessed=4_000_000, transcendentals=0),
        name="finish",
    )(
        places, win_energy.reshape(1, width), slabs, blocks, codes, scales,
        pair_gap.reshape(1, rows), vir_energy.reshape(tiles, tile),
    )


def solution(mesh):
    placed = (
        P("int", "amp", "rep"),
        P("rep", "int", None, None),
        P("rep", "int"),
        P("rep", "int"),
        P("rep", "int"),
        P("rep", "int"),
        P(),
        P("amp"),
        P("rep"),
        P("int"),
    )
    return jax.shard_map(
        local, mesh=mesh, in_specs=placed, out_specs=P("int", "amp", "rep"), check_vma=False
    )
```

time: 57.1 us -> 54 us (0.946)
  the two profiles are of different devices: /device:TPU:2 before, /device:TPU:8 now
where the time goes in v3:
time: 54 us; the launch traced here: 53.8 us
  Pallas kernels  53.8 us (100%)
    pallas_call x1, Pallas kernels, local(): pl.pallas_call(functools.partial(kernel, ny, nz, nx, chains), out_shape=[...  49.6 us
    pallas_call x1, Pallas kernels, local(): pl.pallas_call(finish, out_shape=jax.ShapeDtypeStruct((width, rows, ncol)...  4.16 us

profile of v3, /device:TPU:8, one launch (start us, length us, event | category | flops | bytes accessed | tf_op | source)
XLA Modules:
  0.0 53.8 jit_solution(13786634112508042167)
XLA Ops:
  0.0 49.6 %ladder.1 = (bf16[4,8,128,128]{3,2,1,0:T(8,128)(2,1)}, bf16[4,8,128,128]{3,2,1,0:T(8,128)(2,1)}, s16[2,8,128,128]{3,2,1,0:T(8,128)(2,1)}, f32[2,8,8,128]{3,2,1,0:T(8,128)}, s32[4,2,1,8]{3,2,1,0:T(1,128)}) custom-call(s32[1,8]{1,0:T(1,128)} %st_ref.1, s32[1,8]{1,0:T(1,128)} %sw_ref.1, s32[1,8]{1,0:T(1,128)} %dt_ref.1, s32[1,8]{1,0:T(1,128)} %dw_ref.1, ...), custom_call_target="tpu_custom_call" | custom-call | flops 700000000 | bytes 5000000 | tf_op jit(solution)/shard_map/ladder/pallas_call | solution.py:354
  49.6 4.2 %finish.1 = f32[2,128,1024]{2,1,0:T(8,128)} custom-call(s32[4,2,1,8]{3,2,1,0:T(1,128)} %get-tuple-element.10.idx, f32[1,2]{1,0:T(1,128)} %bitcast.4, bf16[4,8,128,128]{3,2,1,0:T(8,128)(2,1)} %get-tuple-element.11.s_ref, bf16[4,8,128,128]{3,2,1,0:T(8,128)(2,1)} %get-tuple-element.12.b_ref, s16[2,8,128,128]{3,2,1,0:T(8,128)(2,1)} %get-tuple-element.13.y_ref, ...), custom_call_target="tpu_custom_call" | custom-call | flops 140000000 | bytes 4000000 | tf_op jit(solution)/shard_map/finish/pallas_call | solution.py:399

commit v4 on v3

--- a/solution.py
+++ b/solution.py
@@ -11,7 +11,7 @@
 CHUNK = 1
 LEVELS = 32760.0
 LEAST = 1e-33
-SLAB, DUE, APART, DELAY = 0.66, 6.0, 0.6, 2.3
+SLAB, DUE, APART, DELAY = 0.66, 6.0, 1.0, 2.3
 START, COST_Z, COST_F, COST_H = 5.0, 0.12, 0.2, 0.45
 POWER = 0.85
 WINDOW = 4
@@ -93,8 +93,10 @@
         return {"rep": lax.rem(x + (d + nx) % nx, nx)}
 
     sibling = {"int": i + 1 - 2 * core}
-    peers = [ypeer(d) for d in range(1, ny)] + [zpeer(d) for d in range(1, nz)]
-    peers += [xpeer(d) for d in range(1, nx)] + [sibling]
+    far_first = sorted(range(1, ny), key=lambda d: -min(d, ny - d))
+    far_z = sorted(range(1, nz), key=lambda d: -min(d, nz - d))
+    peers = [zpeer(d) for d in far_z] + [sibling] + [ypeer(d) for d in far_first]
+    peers += [xpeer(d) for d in range(1, nx)]
 
     def remote(src, dst, ss, rs, peer):
         return pltpu.make_async_remote_copy(
@@ -143,17 +145,17 @@
         copy.start()
     pl.semaphore_wait(barrier, len(peers))
 
-    far_z = sorted(range(1, nz), key=lambda d: -min(d, nz - d))
-    idx_z = [
-        remote(lists[n], idxs.at[z, n], idx_ss.at[n, d], idx_rs.at[n, d], zpeer(d)) for d in far_z for n in (0, 1)
-    ]
+    idx_z = {
+        d: [remote(lists[n], idxs.at[z, n], idx_ss.at[n, d], idx_rs.at[n, d], zpeer(d)) for n in (0, 1)] for d in far_z
+    }
     idx_x = [
         remote(lists[2 + n], i_out.at[x, n], idx_ss.at[n, nz + d], idx_rs.at[n, nz + d], xpeer(d))
         for d in range(1, nx)
         for n in (0, 1)
     ]
-    for copy in idx_z:
-        send(copy)
+    for pair in idx_z.values():
+        for copy in pair:
+            send(copy)
     twin = []
     for t in range(tiles):
         part = achip.at[t, pl.ds(core * width, width)]
@@ -161,7 +163,6 @@
             remote(amp_ref.at[:, :, t * tile : (t + 1) * tile], part, sib_sem.at[0, t], sib_sem.at[1, t], sibling)
         )
         send(twin[t])
-    far_first = sorted(range(1, ny), key=lambda d: -min(d, ny - d))
     first = {}
     for b in range(width):
         for d in far_first:
@@ -180,8 +181,6 @@
     for copy in shared:
         send(copy)
 
-    for copy in idx_z:
-        copy.wait_recv()
     for copy in own_tab[:2]:
         copy.wait()
     for t in range(tiles):
@@ -200,6 +199,8 @@
         far = hops(direction, chain, nz)
         sign = 1 - 2 * direction
         dest = lax.rem(z + (sign * (far - hop) + nz) % nz, nz)
+        for copy in idx_z.pop((sign * (hop - far) + nz) % nz, ()):
+            copy.wait_recv()
         if hop == 0:
             buf = zinj.at[direction, chain]
         else:
@@ -286,7 +287,7 @@
         copy.wait_send()
 
 
-def finish(idx, win, s_ref, b_ref, y_ref, r_ref, gap_ref, vir_ref, out_ref, s, b, y, r, gap, vir, acc, out, sem):
+def finish(idx_ref, win_ref, s_ref, b_ref, y_ref, r_ref, gap_ref, vir_ref, out_ref, s, b, y, r, gap, vir, acc, inv, out, idx, win, sem, more):
     origins, slots, rows, tile = s.shape
     width, tiles = y.shape[:2]
     x = lax.axis_index("rep")
@@ -294,6 +295,9 @@
         pltpu.make_async_copy(here, there, sem.at[n])
         for n, (here, there) in enumerate(((gap_ref, gap), (vir_ref, vir), (y_ref, y), (r_ref, r)))
     ]
+    first += [
+        pltpu.make_async_copy(here, there, more.at[n]) for n, (here, there) in enumerate(((idx_ref, idx), (win_ref, win)))
+    ]
     blocks = [
         [
             pltpu.make_async_copy(s_ref.at[o], s.at[o], sem.at[4 + 2 * o]),
@@ -303,8 +307,13 @@
     ]
     for copy in first + [copy for pair in blocks for copy in pair]:
         copy.start()
-    for o in range(width * tiles + 1):
-        acc[o] = jnp.zeros((rows, tile), jnp.float32)
+    for copy in first:
+        copy.wait()
+    column = jnp.transpose(jnp.broadcast_to(gap[...], (rows, tile)))
+    for n in range(width):
+        for t in range(tiles):
+            acc[n * tiles + t] = y[n, t].astype(jnp.int32).astype(jnp.float32) * r[n, t, 0:1, :]
+            inv[n * tiles + t] = 1.0 / (win[0, n] + column + vir[t : t + 1, :])
     for o in range(origins):
         for copy in blocks[o]:
             copy.wait()
@@ -313,16 +322,16 @@
             inside = (idx[o, 0, 0, k] >= x * tiles) & (idx[o, 0, 0, k] < (x + 1) * tiles)
             place = jnp.where(inside, place, width * tiles)
             acc[place] += jnp.dot(s[o, k], b[o, k], preferred_element_type=jnp.float32)
-    for copy in first:
-        copy.wait()
-    column = jnp.transpose(jnp.broadcast_to(gap[...], (rows, tile)))
     done = []
     for n in range(width):
         for t in range(tiles):
-            value = y[n, t].astype(jnp.int32).astype(jnp.float32) * r[n, t, 0:1, :] + acc[n * tiles + t]
-            out[n, :, t * tile : (t + 1) * tile] = value / (win[0, n] + column + vir[t : t + 1, :])
-        done.append(pltpu.make_async_copy(out.at[n], out_ref.at[n], sem.at[4 + 2 * origins + n]))
-        done[n].start()
+            out[n, :, t * tile : (t + 1) * tile] = acc[n * tiles + t] * inv[n * tiles + t]
+        for half in range(2):
+            part = pl.ds(half * rows // 2, rows // 2)
+            done.append(
+                pltpu.make_async_copy(out.at[n, part], out_ref.at[n, part], sem.at[4 + 2 * origins + 2 * n + half])
+            )
+            done[-1].start()
     for copy in done:
         copy.wait()
 
@@ -350,7 +359,6 @@
     bf, f32, i32 = jnp.bfloat16, jnp.float32, jnp.int32
     dma = pltpu.SemaphoreType.DMA
     hbm = pl.BlockSpec(memory_space=pltpu.HBM)
-    smem = pl.BlockSpec(memory_space=pltpu.SMEM)
     slabs, blocks, codes, scales, places = pl.pallas_call(
         functools.partial(kernel, ny, nz, nx, chains),
         out_shape=[
@@ -399,7 +407,7 @@
     return pl.pallas_call(
         finish,
         out_shape=jax.ShapeDtypeStruct((width, rows, ncol), f32),
-        in_specs=[smem, smem] + [hbm] * 6,
+        in_specs=[hbm] * 8,
         out_specs=hbm,
         scratch_shapes=[
             pltpu.VMEM(slabs.shape, bf),
@@ -409,8 +417,12 @@
             pltpu.VMEM((1, rows), f32),
             pltpu.VMEM((tiles, tile), f32),
             pltpu.VMEM((width * tiles + 1, rows, tile), f32),
+            pltpu.VMEM((width * tiles, rows, tile), f32),
             pltpu.VMEM((width, rows, ncol), f32),
-            dma((4 + 2 * nx + width,)),
+            pltpu.SMEM((nx, 2, 1, slots), i32),
+            pltpu.SMEM((1, width), f32),
+            dma((4 + 2 * nx + 2 * width,)),
+            dma((2,)),
         ],
         compiler_params=pltpu.CompilerParams(vmem_limit_bytes=60 * 1024 * 1024),
         cost_estimate=pl.CostEstimate(flops=140_000_000, bytes_accessed=4_000_000, transcendentals=0),

time: 54 us -> 52.6 us (0.974)
  Pallas kernels: 53.8 us -> 52.5 us
    pallas_call x1, Pallas kernels: 4.16 us -> 3.43 us  [local(): pl.pallas_call(finish, out_shape=jax.ShapeDtypeStruct((width, rows, ncol)...]
    pallas_call x1, Pallas kernels: 49.6 us -> 49 us  [local(): pl.pallas_call(functools.partial(kernel, ny, nz, nx, chains), out_shape=[...]
where the time goes in v4:
time: 52.6 us; the launch traced here: 52.5 us
  Pallas kernels  52.5 us (100%)
    pallas_call x1, Pallas kernels, local(): pl.pallas_call(functools.partial(kernel, ny, nz, nx, chains), out_shape=[...  49 us
    pallas_call x1, Pallas kernels, local(): pl.pallas_call(finish, out_shape=jax.ShapeDtypeStruct((width, rows, ncol)...  3.43 us

profile of v4, /device:TPU:8, one launch (start us, length us, event | category | flops | bytes accessed | tf_op | source)
XLA Modules:
  0.0 52.5 jit_solution(9702438502384910787)
XLA Ops:
  0.0 49.0 %ladder.1 = (bf16[4,8,128,128]{3,2,1,0:T(8,128)(2,1)}, bf16[4,8,128,128]{3,2,1,0:T(8,128)(2,1)}, s16[2,8,128,128]{3,2,1,0:T(8,128)(2,1)}, f32[2,8,8,128]{3,2,1,0:T(8,128)}, s32[4,2,1,8]{3,2,1,0:T(1,128)}) custom-call(s32[1,8]{1,0:T(1,128)} %st_ref.1, s32[1,8]{1,0:T(1,128)} %sw_ref.1, s32[1,8]{1,0:T(1,128)} %dt_ref.1, s32[1,8]{1,0:T(1,128)} %dw_ref.1, ...), custom_call_target="tpu_custom_call" | custom-call | flops 700000000 | bytes 5000000 | tf_op jit(solution)/shard_map/ladder/pallas_call | solution.py:362
  49.0 3.4 %finish.1 = f32[2,128,1024]{2,1,0:T(8,128)} custom-call(s32[4,2,1,8]{3,2,1,0:T(1,128)} %get-tuple-element.10.idx_ref, f32[1,2]{1,0:T(1,128)} %bitcast.4, bf16[4,8,128,128]{3,2,1,0:T(8,128)(2,1)} %get-tuple-element.11.s_ref, bf16[4,8,128,128]{3,2,1,0:T(8,128)(2,1)} %get-tuple-element.12.b_ref, s16[2,8,128,128]{3,2,1,0:T(8,128)(2,1)} %get-tuple-element.13.y_ref, ...), custom_call_target="tpu_custom_call" | custom-call | flops 140000000 | bytes 4000000 | tf_op jit(solution)/shard_map/finish/pallas_call | solution.py:407

commit v5 on v4

--- a/solution.py
+++ b/solution.py
@@ -11,7 +11,7 @@
 CHUNK = 1
 LEVELS = 32760.0
 LEAST = 1e-33
-SLAB, DUE, APART, DELAY = 0.66, 6.0, 1.0, 2.3
+SLAB, DUE, APART, DELAY = 0.66, 6.0, 1.2, 2.5
 START, COST_Z, COST_F, COST_H = 5.0, 0.12, 0.2, 0.45
 POWER = 0.85
 WINDOW = 4
@@ -69,7 +69,7 @@
     ny, nz, nx, chains,
     st_ref, sw_ref, dt_ref, dw_ref, amp_ref, blk_ref, h_ref,
     s_out, b_out, y_out, r_out, i_out,
-    achip, x_in, hv, sall, zinj, zbuf, idxs, ysend, ssend,
+    achip, x_in, hv, sall, zinj, zbuf, idxs, ysend, ssend, own,
     tab_sem, amp_sem, loc_sem, own_sem, sib_sem, idx_ss, idx_rs, y1_ss, y1_rs, y2_ss, y2_rs, z_ss, z_rs, b_ss, b_rs, s_ss, s_rs,
 ):
     width, rows, ncol = amp_ref.shape
@@ -134,7 +134,7 @@
         for t in range(tiles)
     ]
     own_h = pltpu.make_async_copy(h_ref, hv, loc_sem.at[1])
-    own_blk = pltpu.make_async_copy(blk_ref.at[0], b_out.at[x], loc_sem.at[2])
+    own_blk = pltpu.make_async_copy(blk_ref.at[0], own, loc_sem.at[2])
     own_x = [
         pltpu.make_async_copy(
             amp_ref.at[b, :, span(y, tile)], x_in.at[b, span(y, rows), :], loc_sem.at[3 + b]
@@ -181,8 +181,9 @@
     for copy in shared:
         send(copy)
 
-    for copy in own_tab[:2]:
+    for copy in own_tab[:2] + [own_blk]:
         copy.wait()
+    keep(pltpu.make_async_copy(own, b_out.at[x], loc_sem.at[7]))
     for t in range(tiles):
         own_amp[t].wait()
         twin[t].wait_recv()
@@ -278,7 +279,6 @@
     runs = {"z": z_message, "f": z_final, "h": lambda b, n: hole(b, (far_first + [0])[n])}
     for kind, *place in plan(nz, chains, width, ny):
         runs[kind](*place)
-    own_blk.wait()
     for copy in own_tab[2:] + kept:
         copy.wait()
     for copy in idx_x + shared + list(spread.values()) + [copy for pair in second.values() for copy in pair]:
@@ -287,7 +287,7 @@
         copy.wait_send()
 
 
-def finish(idx_ref, win_ref, s_ref, b_ref, y_ref, r_ref, gap_ref, vir_ref, out_ref, s, b, y, r, gap, vir, acc, inv, out, idx, win, sem, more):
+def finish(idx_ref, win_ref, s_ref, b_ref, y_ref, r_ref, gap_ref, vir_ref, out_ref, s, b, y, r, gap, vir, acc, inv, out, idx, win, sem, more, out_sem):
     origins, slots, rows, tile = s.shape
     width, tiles = y.shape[:2]
     x = lax.axis_index("rep")
@@ -310,6 +310,7 @@
     for copy in first:
         copy.wait()
     column = jnp.transpose(jnp.broadcast_to(gap[...], (rows, tile)))
+    acc[width * tiles] = jnp.zeros((rows, tile), jnp.float32)
     for n in range(width):
         for t in range(tiles):
             acc[n * tiles + t] = y[n, t].astype(jnp.int32).astype(jnp.float32) * r[n, t, 0:1, :]
@@ -325,12 +326,9 @@
     done = []
     for n in range(width):
         for t in range(tiles):
-            out[n, :, t * tile : (t + 1) * tile] = acc[n * tiles + t] * inv[n * tiles + t]
-        for half in range(2):
-            part = pl.ds(half * rows // 2, rows // 2)
-            done.append(
-                pltpu.make_async_copy(out.at[n, part], out_ref.at[n, part], sem.at[4 + 2 * origins + 2 * n + half])
-            )
+            o = n * tiles + t
+            out[o] = acc[o] * inv[o]
+            done.append(pltpu.make_async_copy(out.at[o], out_ref.at[n, :, t * tile : (t + 1) * tile], out_sem.at[o]))
             done[-1].start()
     for copy in done:
         copy.wait()
@@ -380,6 +378,7 @@
             pltpu.SMEM((nz, 2, 1, slots), i32),
             pltpu.VMEM((width, ny, rows, tile), jnp.int16),
             pltpu.VMEM((width, ny, 8, tile), f32),
+            pltpu.VMEM((slots, tile, tile), bf),
             dma((4,)),
             dma((tiles,)),
             dma((8,)),
@@ -418,11 +417,12 @@
             pltpu.VMEM((tiles, tile), f32),
             pltpu.VMEM((width * tiles + 1, rows, tile), f32),
             pltpu.VMEM((width * tiles, rows, tile), f32),
-            pltpu.VMEM((width, rows, ncol), f32),
+            pltpu.VMEM((width * tiles, rows, tile), f32),
             pltpu.SMEM((nx, 2, 1, slots), i32),
             pltpu.SMEM((1, width), f32),
-            dma((4 + 2 * nx + 2 * width,)),
+            dma((4 + 2 * nx,)),
             dma((2,)),
+            dma((width * tiles,)),
         ],
         compiler_params=pltpu.CompilerParams(vmem_limit_bytes=60 * 1024 * 1024),
         cost_estimate=pl.CostEstimate(flops=140_000_000, bytes_accessed=4_000_000, transcendentals=0),

time: 52.6 us -> 52.5 us (level)
  no operation moved by 1% of the time
where the time goes in v5:
time: 52.5 us; the launch traced here: 52.4 us
  Pallas kernels  52.4 us (100%)
    pallas_call x1, Pallas kernels, local(): pl.pallas_call(functools.partial(kernel, ny, nz, nx, chains), out_shape=[...  48.9 us
    pallas_call x1, Pallas kernels, local(): pl.pallas_call(finish, out_shape=jax.ShapeDtypeStruct((width, rows, ncol)...  3.49 us

profile of v5, /device:TPU:8, one launch (start us, length us, event | category | flops | bytes accessed | tf_op | source)
XLA Modules:
  0.0 52.4 jit_solution(17413843684069279478)
XLA Ops:
  0.0 48.9 %ladder.1 = (bf16[4,8,128,128]{3,2,1,0:T(8,128)(2,1)}, bf16[4,8,128,128]{3,2,1,0:T(8,128)(2,1)}, s16[2,8,128,128]{3,2,1,0:T(8,128)(2,1)}, f32[2,8,8,128]{3,2,1,0:T(8,128)}, s32[4,2,1,8]{3,2,1,0:T(1,128)}) custom-call(s32[1,8]{1,0:T(1,128)} %st_ref.1, s32[1,8]{1,0:T(1,128)} %sw_ref.1, s32[1,8]{1,0:T(1,128)} %dt_ref.1, s32[1,8]{1,0:T(1,128)} %dw_ref.1, ...), custom_call_target="tpu_custom_call" | custom-call | flops 700000000 | bytes 5000000 | tf_op jit(solution)/shard_map/ladder/pallas_call | solution.py:360
  48.9 3.5 %finish.1 = f32[2,128,1024]{2,1,0:T(8,128)} custom-call(s32[4,2,1,8]{3,2,1,0:T(1,128)} %get-tuple-element.10.idx_ref, f32[1,2]{1,0:T(1,128)} %bitcast.4, bf16[4,8,128,128]{3,2,1,0:T(8,128)(2,1)} %get-tuple-element.11.s_ref, bf16[4,8,128,128]{3,2,1,0:T(8,128)(2,1)} %get-tuple-element.12.b_ref, s16[2,8,128,128]{3,2,1,0:T(8,128)(2,1)} %get-tuple-element.13.y_ref, ...), custom_call_target="tpu_custom_call" | custom-call | flops 140000000 | bytes 4000000 | tf_op jit(solution)/shard_map/finish/pallas_call | solution.py:406

commit v6 on v5

--- a/solution.py
+++ b/solution.py
@@ -14,7 +14,7 @@
 SLAB, DUE, APART, DELAY = 0.66, 6.0, 1.2, 2.5
 START, COST_Z, COST_F, COST_H = 5.0, 0.12, 0.2, 0.45
 POWER = 0.85
-WINDOW = 4
+WINDOW = 5
 
 
 def hops(direction, chain, nz):

time: 52.5 us -> 52.5 us (level)
  no operation moved by 1% of the time
where the time goes in v6:
time: 52.5 us; the launch traced here: 52.3 us
  Pallas kernels  52.3 us (100%)
    pallas_call x1, Pallas kernels, local(): pl.pallas_call(functools.partial(kernel, ny, nz, nx, chains), out_shape=[...  48.9 us
    pallas_call x1, Pallas kernels, local(): pl.pallas_call(finish, out_shape=jax.ShapeDtypeStruct((width, rows, ncol)...  3.46 us

profile of v6, /device:TPU:8, one launch (start us, length us, event | category | flops | bytes accessed | tf_op | source)
XLA Modules:
  0.0 52.3 jit_solution(13436782149476826236)
XLA Ops:
  0.0 48.9 %ladder.1 = (bf16[4,8,128,128]{3,2,1,0:T(8,128)(2,1)}, bf16[4,8,128,128]{3,2,1,0:T(8,128)(2,1)}, s16[2,8,128,128]{3,2,1,0:T(8,128)(2,1)}, f32[2,8,8,128]{3,2,1,0:T(8,128)}, s32[4,2,1,8]{3,2,1,0:T(1,128)}) custom-call(s32[1,8]{1,0:T(1,128)} %st_ref.1, s32[1,8]{1,0:T(1,128)} %sw_ref.1, s32[1,8]{1,0:T(1,128)} %dt_ref.1, s32[1,8]{1,0:T(1,128)} %dw_ref.1, ...), custom_call_target="tpu_custom_call" | custom-call | flops 700000000 | bytes 5000000 | tf_op jit(solution)/shard_map/ladder/pallas_call | solution.py:360
  48.9 3.5 %finish.1 = f32[2,128,1024]{2,1,0:T(8,128)} custom-call(s32[4,2,1,8]{3,2,1,0:T(1,128)} %get-tuple-element.10.idx_ref, f32[1,2]{1,0:T(1,128)} %bitcast.4, bf16[4,8,128,128]{3,2,1,0:T(8,128)(2,1)} %get-tuple-element.11.s_ref, bf16[4,8,128,128]{3,2,1,0:T(8,128)(2,1)} %get-tuple-element.12.b_ref, s16[2,8,128,128]{3,2,1,0:T(8,128)(2,1)} %get-tuple-element.13.y_ref, ...), custom_call_target="tpu_custom_call" | custom-call | flops 140000000 | bytes 4000000 | tf_op jit(solution)/shard_map/finish/pallas_call | solution.py:406
